TPU v7x, 512 devices: a whole 4x4x16 slice. The times are simulated.
512 devices in a mesh: blk: 64 (over x, z_lo, core), tp: 8 (over z_hi, y).
Axes of the slice: x: 4, y: 4, z: 16 (z_hi: 2, z_lo: 8; z = z_hi * 8 + z_lo), core: 2. Of those that a mesh axis runs over, the one named last changes fastest.
Arguments:
- weights: float32 [64, 1024, 1024], P('blk', None, 'tp'), may hold values from -6 to 6
- copies: bfloat16 [64, 1024, 1024], P('blk', None, 'tp'), may hold values from -60 to 60
- copies_mixed: bfloat16 [64, 1024, 1024], P('blk', None, 'tp'), may hold values from -64 to 64
- tracker: bfloat16 [64, 1024, 1024], P('blk', None, 'tp'), may hold values from -6 to 6
- tracker_copy: bfloat16 [64, 1024, 1024], P('blk', None, 'tp'), may hold values from -6 to 6
- tracker_mixed: bfloat16 [64, 1024, 1024], P('blk', None, 'tp'), may hold values from -6 to 6
- grad_prev: bfloat16 [64, 1024, 1024], P('blk', None, 'tp'), may hold values from -3 to 3
- tokens: bfloat16 [64, 1024, 1024], P('blk', 'tp'), may hold values from -12 to 12
- image_ids: int32 [64, 1024], P('blk'), may hold values from 0 to 5, never falling along the last dimension, each value on 1 to 197 neighbouring positions
- key_weight: bfloat16 [1024, 1024], P(None, 'tp'), may hold values from -0.1875 to 0.1875
- value_weight: bfloat16 [1024, 1024], P(None, 'tp'), may hold values from -0.1875 to 0.1875
- out_grad: bfloat16 [64, 1024, 1024], P('blk', None, 'tp'), may hold values from -48 to 48
- row_picks: int32 [64, 2, 64], replicated, may hold values from 0 to 1023, as said below
Outputs:
- weights_new: float32 [64, 1024, 1024], P('blk', None, 'tp')
- copies_new: bfloat16 [64, 1024, 1024], P('blk', None, 'tp')
- mixed_new: bfloat16 [64, 1024, 1024], P('blk', None, 'tp')
- tracker_new: bfloat16 [64, 1024, 1024], P('blk', None, 'tp')
- tracker_copy_new: bfloat16 [64, 1024, 1024], P('blk', None, 'tp')
- tracker_mixed_new: bfloat16 [64, 1024, 1024], P('blk', None, 'tp')
- grad_new: bfloat16 [64, 1024, 1024], P('blk', None, 'tp')
- consensus: float32 [], replicated
Inputs may be any that keep to these rules, and one draw needn't show every extreme that they name: `image_ids`: never falling along a replica's tokens; an image holds 1 to 197 tokens. `row_picks`: each row lists 64 different rows; the same picks serve every head shard of a replica.
All inputs are finite; a program needn't handle non-finite values.
Results may differ from a plain program's by a relative error of at most 0.0095.
The roundings to bfloat16 on the way count: a program that leaves them out, or rounds other values in their place, can miss the bound.
Values may be sent and summed in bfloat16 or wider, within the bound.
No kernel may reach another device: no remote copies, remote signals or barrier semaphores. Data moves between devices by JAX's collectives and lax.ppermute only.
A program may use at most 64 MiB of HBM per device.

v0:
```python
import jax
import jax.numpy as jnp
from jax import lax
from jax.sharding import Mesh
from jax.sharding import PartitionSpec as P

HD = 64
BLK = ("blk_0", "blk_1", "blk_2")
BLK_TP = ("blk_0", "blk_1", "blk_2", "tp_0", "tp_1")
TP = ("tp_0", "tp_1")
mixing_rate = 0.2
step_rate = 0.5


def over_axes(value, axes):
    for axis in axes:
        value = lax.psum(value, axis)
    return value


def extended(value, sides, width):
    for axis, dim in sides:
        size, length = (lax.axis_size(axis), value.shape[dim])
        up = [(i, (i + 1) % size) for i in range(size)]
        down = [(j, i) for i, j in up]
        last = lax.slice_in_dim(value, length - width, length, axis=dim)
        leading = lax.slice_in_dim(value, 0, width, axis=dim)
        before = lax.ppermute(last, axis, up)
        after = lax.ppermute(leading, axis, down)
        value = jnp.concatenate([before, value, after], axis=dim)
    return value


def contract(left, right, left_dim, right_dim):
    return lax.dot_general(
        left, right, (((left_dim,), (right_dim,)), ((), ())), preferred_element_type=jnp.float32
    )


def pick_matrix(picks, total_rows):
    columns = lax.broadcasted_iota(jnp.int32, (picks.shape[0], total_rows), 1)
    return (picks[:, None] == columns).astype(jnp.float32)


def select_rows(picks, field):
    return jnp.dot(pick_matrix(picks, field.shape[0]), field, precision=lax.Precision.HIGHEST)


def place_rows(picks, values, total_rows):
    matrix = pick_matrix(picks, total_rows)
    return lax.dot_general(
        matrix, values, (((0,), (0,)), ((), ())), precision=lax.Precision.HIGHEST
    )


def neighbour_picks(row_picks, stream):
    replica_count = lax.axis_size(BLK)
    replica_rank = lax.axis_index(BLK)
    lower_picks = lax.dynamic_index_in_dim(
        row_picks, (replica_rank - 1 + replica_count) % replica_count, 0, keepdims=False
    )[stream]
    own_picks = lax.dynamic_index_in_dim(row_picks, replica_rank, 0, keepdims=False)[stream]
    upper_picks = lax.dynamic_index_in_dim(
        row_picks, (replica_rank + 1) % replica_count, 0, keepdims=False
    )[stream]
    return jnp.concatenate([lower_picks, own_picks, upper_picks], axis=0)


def mix_stream(received, row_picks, stream, total_rows):
    picks = neighbour_picks(row_picks, stream)
    values = received.reshape(received.shape[0] * received.shape[1], received.shape[2])
    return place_rows(picks, values, total_rows) / 3.0


def consensus_of(mixed_new, copies_new):
    gap_value = mixed_new.astype(jnp.float32) - copies_new.astype(jnp.float32)
    local_sum = jnp.sum(gap_value * gap_value)
    total_sum = over_axes(local_sum, BLK_TP)
    count = lax.axis_size(BLK) * copies_new.shape[0] * copies_new.shape[0]
    return total_sum / float(count)


def head_grad(query_head, key_head, value_head, out_head, same_image):
    scores = contract(query_head, key_head, 1, 1) * HD ** (-0.5)
    scores = jnp.where(same_image, scores, -1e30)
    row_max = jnp.max(scores, axis=-1, keepdims=True)
    exponent = jnp.exp(scores - row_max)
    attention = exponent / jnp.sum(exponent, axis=-1, keepdims=True)
    out_proj = contract(out_head, value_head, 1, 1)
    centred = out_proj - jnp.sum(attention * out_proj, axis=-1, keepdims=True)
    score_grad = (attention * centred * HD ** (-0.5)).astype(jnp.bfloat16)
    return jnp.dot(score_grad, key_head, preferred_element_type=jnp.float32).astype(jnp.bfloat16)


def attention_grad(projected, image_row, out_rows):
    width = out_rows.shape[1]
    queries = projected[:, :width]
    keyed = projected[:, width : 2 * width]
    valued = projected[:, 2 * width :]
    same_image = image_row[:, None] == image_row[None, :]
    pieces_list = []
    for head_index in range(width // HD):
        low_col = head_index * HD
        pieces_list.append(
            head_grad(
                queries[:, low_col : low_col + HD],
                keyed[:, low_col : low_col + HD],
                valued[:, low_col : low_col + HD],
                out_rows[:, low_col : low_col + HD],
                same_image,
            )
        )
    return jnp.concatenate(pieces_list, axis=1)


def local_gradient(weights_new, tokens, image_ids, key_weight, value_weight, out_grad):
    model_width = weights_new.shape[0]
    query_weight = (weights_new * model_width ** (-0.5)).astype(jnp.bfloat16)
    joined = jnp.concatenate([query_weight, key_weight, value_weight], axis=1)
    gathered = lax.all_gather(tokens, TP, axis=1, tiled=True)
    projected = jnp.dot(gathered[0], joined, preferred_element_type=jnp.float32).astype(
        jnp.bfloat16
    )[None][0]
    query_grad = attention_grad(projected, image_ids[0], out_grad[0])
    total = contract(gathered[0], query_grad, 0, 0)
    return (total * model_width ** (-0.5)).astype(jnp.bfloat16)


def per_device(
    weights,
    copies,
    copies_mixed,
    tracker,
    tracker_copy,
    tracker_mixed,
    grad_prev,
    tokens,
    image_ids,
    key_weight,
    value_weight,
    out_grad,
    row_picks,
):
    model_width = weights.shape[1]
    replica_rank = lax.axis_index(BLK)
    own_picks = lax.dynamic_index_in_dim(row_picks, replica_rank, 0, keepdims=False)
    copy_value = copies[0].astype(jnp.float32)
    mixed_value = copies_mixed[0].astype(jnp.float32)
    weights_new = (
        weights[0]
        + mixing_rate * (mixed_value - copy_value)
        - step_rate * tracker[0].astype(jnp.float32)
    )
    param_values = select_rows(own_picks[0], weights_new - copy_value)
    copies_new = (copy_value + place_rows(own_picks[0], param_values, model_width)).astype(
        jnp.bfloat16
    )
    param_received = extended(param_values[None].astype(jnp.bfloat16), ((BLK, 0),), 1).astype(
        jnp.float32
    )
    mixed_new = (mixed_value + mix_stream(param_received, row_picks, 0, model_width)).astype(
        jnp.bfloat16
    )
    consensus = consensus_of(mixed_new, copies_new)
    grad_new = local_gradient(weights_new, tokens, image_ids, key_weight, value_weight, out_grad)
    tracker_copy_value = tracker_copy[0].astype(jnp.float32)
    tracker_mixed_value = tracker_mixed[0].astype(jnp.float32)
    tracker_new = (
        tracker[0].astype(jnp.float32)
        + mixing_rate * (tracker_mixed_value - tracker_copy_value)
        + grad_new.astype(jnp.float32)
        - grad_prev[0].astype(jnp.float32)
    ).astype(jnp.bfloat16)
    tracker_values = select_rows(own_picks[1], tracker_new.astype(jnp.float32) - tracker_copy_value)
    tracker_copy_new = (
        tracker_copy_value + place_rows(own_picks[1], tracker_values, model_width)
    ).astype(jnp.bfloat16)
    tracker_received = extended(tracker_values[None], ((BLK, 0),), 1)
    tracker_mixed_new = (
        tracker_mixed_value + mix_stream(tracker_received, row_picks, 1, model_width)
    ).astype(jnp.bfloat16)
    return (
        weights_new[None],
        copies_new[None],
        mixed_new[None],
        tracker_new[None],
        tracker_copy_new[None],
        tracker_mixed_new[None],
        grad_new[None],
        consensus,
    )


def solution(mesh):
    finer = Mesh(mesh.devices.reshape(4, 8, 2, 2, 4), ("blk_0", "blk_1", "blk_2", "tp_0", "tp_1"))
    in_specs = (
        P(BLK, None, TP),
        P(BLK, None, TP),
        P(BLK, None, TP),
        P(BLK, None, TP),
        P(BLK, None, TP),
        P(BLK, None, TP),
        P(BLK, None, TP),
        P(BLK, TP, None),
        P(BLK, None),
        P(None, TP),
        P(None, TP),
        P(BLK, None, TP),
        P(),
    )
    out_specs = (
        P(BLK, None, TP),
        P(BLK, None, TP),
        P(BLK, None, TP),
        P(BLK, None, TP),
        P(BLK, None, TP),
        P(BLK, None, TP),
        P(BLK, None, TP),
        P(),
    )
    return jax.shard_map(
        per_device, mesh=finer, in_specs=in_specs, out_specs=out_specs, check_vma=False
    )
```

profile of v0, /device:TPU:8, one launch (start us, length us, event | category | flops | bytes accessed | tf_op | source)
XLA Modules:
  0.0 177.8 jit_solution(13009544344436294952)
XLA Ops:
  7.2 0.0 copy-start
  7.2 0.0 copy-start.3
  7.2 0.0 copy-start.4
  7.2 0.0 copy-start.1
  7.2 0.0 all-gather.2.cloned.1.call-start
  7.3 0.7 all-gather.2.cloned.1.call-update
  8.0 0.7 constant_dynamic-slice_fusion.1
  8.7 1.8 fusion.64
  10.5 1.9 %collective-permute-start = (bf16[1,64,128]{2,1,0:T(8,128)(2,1)S(1)}, bf16[1,64,128]{2,1,0:T(8,128)(2,1)S(1)}, u32[]{:S(2)}, u32[]{:S(2)}) collective-permute-start(bf16[1,64,128]{2,1,0:T(8,128)(2,1)S(1)} %convert_bitcast_fusion.3), channel_id=1, source_target_pairs={{0,8},{8,16},{16,24},{24,32},{32,40},{40,48},{48,56},{56,64},{64,7... | collective-permute-start | bytes 49160 | tf_op jit(solution)/shard_map/ppermute | solution.py:28
  12.4 14.8 %collective-permute-start.1 = (bf16[1,64,128]{2,1,0:T(8,128)(2,1)S(1)}, bf16[1,64,128]{2,1,0:T(8,128)(2,1)S(1)}, u32[]{:S(2)}, u32[]{:S(2)}) collective-permute-start(bf16[1,64,128]{2,1,0:T(8,128)(2,1)S(1)} %convert_bitcast_fusion.3), channel_id=1, source_target_pairs={{8,0},{16,8},{24,16},{32,24},{40,32},{48,40},{56,48},{64,56},{72,6... | collective-permute-start | bytes 49160 | tf_op jit(solution)/shard_map/ppermute | solution.py:29
  27.3 0.1 pad_add_fusion
  27.3 0.0 collective-permute-done
  27.3 1.3 collective-permute-done.1
  28.7 1.5 fusion.38
  30.2 0.0 copy-start.13
  30.2 3.0 %multiply_reduce_fusion = (f32[]{:T(128)}, bf16[1024,128]{1,0:T(8,128)(2,1)}) fusion(bf16[1024,128]{1,0:T(8,128)(2,1)S(1)} %fusion.38, f32[64,128]{1,0:T(8,128)S(1)} %fusion.64, s32[64]{0:T(128)S(1)} %get-tuple-element.22, bf16[1,1024,128]{2,1,0:T(8,128)(2,1)} %param.14), kind=kOutput, calls=%fused_computation.80 | convolution fusion | flops 101777408 | bytes 819460 | tf_op jit(solution)/shard_map/dot_general | solution.py:51
  33.2 9.2 %psum.35 = f32[]{:T(128)} all-reduce(f32[]{:T(128)} %get-tuple-element.27), channel_id=1, replica_groups=mesh['blk_0'=4,'blk_1'=8,'blk_2'=2,'tp_0'=2,'tp_1'=4] {'blk_0'}, use_global_device_ids=true, to_apply=%region_7.8 | all-reduce | flops 1 | bytes 8 | tf_op jit(solution)/shard_map/psum | solution.py:17
  42.4 27.7 %psum.36 = f32[]{:T(128)} all-reduce(f32[]{:T(128)} %psum.35), channel_id=1, replica_groups=mesh['blk_0'=4,'blk_1'=8,'blk_2'=2,'tp_0'=2,'tp_1'=4] {'blk_1'}, use_global_device_ids=true, to_apply=%region_8.9 | all-reduce | flops 1 | bytes 8 | tf_op jit(solution)/shard_map/psum | solution.py:17
  70.1 2.3 %fusion.68 = f32[1,1024,128]{2,1,0:T(8,128)} fusion(f32[1,1024,128]{2,1,0:T(8,128)} %param.13, bf16[1,1024,128]{2,1,0:T(8,128)(2,1)} %param.14, bf16[1,1024,128]{2,1,0:T(8,128)(2,1)} %param.15, bf16[1,1024,128]{2,1,0:T(8,128)(2,1)} %param.16), kind=kLoop, calls=%fused_computation.74 | loop fusion | flops 1048576 | bytes 1835008 | tf_op jit(solution)/shard_map/sub | solution.py:150
  72.4 5.8 %psum.37 = f32[]{:T(128)} all-reduce(f32[]{:T(128)} %psum.36), channel_id=1, replica_groups=mesh['blk_0'=4,'blk_1'=8,'blk_2'=2,'tp_0'=2,'tp_1'=4] {'blk_2'}, use_global_device_ids=true, to_apply=%region_9.10 | all-reduce | flops 1 | bytes 8 | tf_op jit(solution)/shard_map/psum | solution.py:17
  78.2 0.2 multiply_convert_fusion
  78.4 25.9 %psum.38 = f32[]{:T(128)} all-reduce(f32[]{:T(128)} %psum.37), channel_id=1, replica_groups=mesh['blk_0'=4,'blk_1'=8,'blk_2'=2,'tp_0'=2,'tp_1'=4] {'tp_0'}, use_global_device_ids=true, to_apply=%region_10.11 | all-reduce | flops 1 | bytes 8 | tf_op jit(solution)/shard_map/psum | solution.py:17
  104.3 0.1 pad_add_fusion.1
  104.4 9.3 %psum.39 = f32[]{:T(128)} all-reduce(f32[]{:T(128)} %psum.38), channel_id=1, replica_groups=mesh['blk_0'=4,'blk_1'=8,'blk_2'=2,'tp_0'=2,'tp_1'=4] {'tp_1'}, use_global_device_ids=true, to_apply=%region_11.12 | all-reduce | flops 1 | bytes 8 | tf_op jit(solution)/shard_map/psum | solution.py:17
  114.3 0.0 copy-start.7
  114.3 21.1 %all-gather.2.cloned.1.call-done = bf16[1,1024,1024]{2,1,0:T(8,128)(2,1)} async-done(((bf16[1,128,1024]{2,1,0:T(8,128)(2,1)}), bf16[1,1024,1024]{2,1,0:T(8,128)(2,1)}) %all-gather.2.cloned.1.call-update) | async-done | bytes 2097168 | tf_op jit(solution)/shard_map/all_gather | solution.py:120
  135.4 0.0 copy-done.11
  135.4 2.6 %fusion.29 = bf16[1024,384]{0,1:T(8,128)(2,1)S(1)} fusion(bf16[1,1024,1024]{2,1,0:T(8,128)(2,1)} %all-gather.2.cloned.1.call-done, bf16[1024,128]{1,0:T(8,128)(2,1)S(1)} %copy-done.11, bf16[1024,128]{1,0:T(8,128)(2,1)S(1)} %copy-done.12, bf16[1024,128]{1,0:T(8,128)(2,1)S(1)} %multiply_convert_fusion), kind=kOutput, calls=%fused_computation.33 | convolution fusion | flops 808058880 | bytes 3670016 | tf_op jit(solution)/shard_map/dot_general | solution.py:121
  138.0 0.0 copy-start.10
  138.0 0.8 fusion.86
  138.8 0.8 fusion.77
  139.6 0.0 copy-done.10
  139.6 1.3 fusion.12
  140.8 2.4 %fusion.9 = (f32[1024]{0:T(1024)S(1)}, f32[1024]{0:T(1024)S(1)}) fusion(f32[1024,1024]{0,1:T(8,128)S(1)} %get-tuple-element.23, f32[1024]{0:T(1024)S(1)} %get-tuple-element.12, s32[1024]{0:T(1024)S(1)} %bitcast.167, f32[1024]{0:T(1024)S(1)} %get-tuple-element.13, f32[1024,1024]{0,1:T(8,128)S(1)} %fusion.86), kind=kLoop, calls=%fused_computation.17 | loop fusion | flops 9435136 | bytes 8409088 | tf_op jit(solution)/shard_map/reduce_sum | solution.py:88
  143.3 2.7 %fusion.4 = (f32[1024]{0:T(1024)S(1)}, f32[1024]{0:T(1024)S(1)}, f32[1024,1024]{1,0:T(8,128)S(1)}) fusion(f32[1024]{0:T(1024)S(1)} %get-tuple-element.10, f32[1024]{0:T(1024)S(1)} %get-tuple-element.12, f32[1024,1024]{0,1:T(8,128)S(1)} %get-tuple-element.23, s32[1024]{0:T(1024)S(1)} %bitcast.168, f32[1024,1024]{1,0:T(8,128)S(1)} %fusion.77, ...), kind=kOutput, calls=%fused_computation.10 | convolution fusion | flops 147847168 | bytes 17203200 | tf_op jit(solution)/shard_map/dot_general | solution.py:35
  146.0 1.9 %fusion.41 = bf16[1024,64]{1,0:T(8,128)(2,1)S(1)} fusion(f32[1024,1024]{1,0:T(8,128)S(1)} %fusion.77, f32[1024]{0:T(1024)S(1)} %get-tuple-element.9, bf16[1024,384]{0,1:T(8,128)(2,1)S(1)} %fusion.29, f32[1024,1024]{0,1:T(8,128)S(1)} %fusion.86, f32[1024]{0:T(1024)S(1)} %get-tuple-element.11, f32[1024]{0:T(1024)S(1)} %get-tuple-element.13, ...), kind=kOutput, calls=%fused_computation.45 | convolution fusion | flops 143720448 | bytes 8671232 | tf_op jit(solution)/shard_map/dot_general | solution.py:92
  147.9 0.0 copy-start.2
  148.0 0.0 copy-start.8
  148.0 0.0 copy-start.9
  148.0 1.9 %fusion.44 = bf16[1024,64]{1,0:T(8,128)(2,1)S(1)} fusion(f32[1024,1024]{1,0:T(8,128)S(1)} %get-tuple-element.24, f32[1024]{0:T(1024)S(1)} %get-tuple-element.8, bf16[1024,384]{0,1:T(8,128)(2,1)S(1)} %fusion.29, f32[1024,1024]{0,1:T(8,128)S(1)} %get-tuple-element.23, f32[1024]{0:T(1024)S(1)} %get-tuple-element.10, f32[1024]{0:T(1024)S(1)} %get-tuple-element.12, ...), kind=kOutput, calls=%fused_computation.46 | convolution fusion | flops 143720448 | bytes 8671232 | tf_op jit(solution)/shard_map/dot_general | solution.py:92
  150.0 1.8 %fusion.71 = (bf16[1024,128]{1,0:T(8,128)(2,1)S(1)}, bf16[128,1024]{0,1:T(8,128)(2,1)}) fusion(bf16[1,1024,128]{2,1,0:T(8,128)(2,1)S(1)} %copy-done.1, bf16[1,1024,128]{2,1,0:T(8,128)(2,1)S(1)} %copy-done.8, bf16[1,1024,128]{2,1,0:T(8,128)(2,1)S(1)} %copy-done.9, bf16[1,1024,128]{2,1,0:T(8,128)(2,1)S(1)} %copy-done.2, ...), kind=kOutput, calls=%fused_computation.77 | convolution fusion | flops 270663680 | bytes 3932160 | tf_op jit(solution)/shard_map/dot_general | solution.py:35
  151.8 0.4 fusion.73
  152.1 1.9 %collective-permute-start.2 = (f32[1,64,128]{2,1,0:T(8,128)S(1)}, f32[1,64,128]{2,1,0:T(8,128)S(1)}, u32[]{:S(2)}, u32[]{:S(2)}) collective-permute-start(f32[1,64,128]{2,1,0:T(8,128)S(1)} %bitcast.158), channel_id=1, source_target_pairs={{0,8},{8,16},{16,24},{24,32},{32,40},{40,48},{48,56},{56,64},{64,7... | collective-permute-start | bytes 98312 | tf_op jit(solution)/shard_map/ppermute | solution.py:28
  154.1 12.4 %collective-permute-start.3 = (f32[1,64,128]{2,1,0:T(8,128)S(1)}, f32[1,64,128]{2,1,0:T(8,128)S(1)}, u32[]{:S(2)}, u32[]{:S(2)}) collective-permute-start(f32[1,64,128]{2,1,0:T(8,128)S(1)} %bitcast.159), channel_id=1, source_target_pairs={{8,0},{16,8},{24,16},{32,24},{40,32},{48,40},{56,48},{64,56},{72,6... | collective-permute-start | bytes 98312 | tf_op jit(solution)/shard_map/ppermute | solution.py:29
  166.4 1.4 fusion.50
  167.8 0.0 collective-permute-done.2
  167.8 0.2 collective-permute-done.3
  168.0 1.8 %fusion.51 = bf16[1,1024,128]{2,1,0:T(8,128)(2,1)} fusion(f32[192,128]{1,0:T(8,128)S(1)} %bitcast.164, s32[192]{0:T(256)S(1)} %pad_add_fusion.1, bf16[1,1024,128]{2,1,0:T(8,128)(2,1)S(1)} %copy-done.9), kind=kOutput, calls=%fused_computation.49 | convolution fusion | flops 302710784 | bytes 623360 | tf_op jit(solution)/shard_map/dot_general | solution.py:51
  (21 shorter events, 0.1 us)
Async XLA Ops:
  7.2 71.0 %copy-start = (f32[1,1024,128]{2,1,0:T(8,128)S(1)}, f32[1,1024,128]{2,1,0:T(8,128)}, u32[]{:S(2)}) copy-start(f32[1,1024,128]{2,1,0:T(8,128)} %param.13) | copy-start | bytes 1572868
  7.2 71.0 %copy-start.3 = (bf16[1,1024,128]{2,1,0:T(8,128)(2,1)S(1)}, bf16[1,1024,128]{2,1,0:T(8,128)(2,1)}, u32[]{:S(2)}) copy-start(bf16[1,1024,128]{2,1,0:T(8,128)(2,1)} %param.14) | copy-start | bytes 786436
  7.2 71.0 %copy-start.4 = (bf16[1,1024,128]{2,1,0:T(8,128)(2,1)S(1)}, bf16[1,1024,128]{2,1,0:T(8,128)(2,1)}, u32[]{:S(2)}) copy-start(bf16[1,1024,128]{2,1,0:T(8,128)(2,1)} %param.15) | copy-start | bytes 786436
  7.2 71.0 %copy-start.1 = (bf16[1,1024,128]{2,1,0:T(8,128)(2,1)S(1)}, bf16[1,1024,128]{2,1,0:T(8,128)(2,1)}, u32[]{:S(2)}) copy-start(bf16[1,1024,128]{2,1,0:T(8,128)(2,1)} %param.16) | copy-start | bytes 786436
  7.2 128.1 %copy-start.12 = (bf16[1024,128]{1,0:T(8,128)(2,1)S(1)}, bf16[1024,128]{1,0:T(8,128)(2,1)}, u32[]{:S(2)}) copy-start(bf16[1024,128]{1,0:T(8,128)(2,1)} %param.22) | copy-start | bytes 786436
  7.2 128.1 %copy-start.11 = (bf16[1024,128]{1,0:T(8,128)(2,1)S(1)}, bf16[1024,128]{1,0:T(8,128)(2,1)}, u32[]{:S(2)}) copy-start(bf16[1024,128]{1,0:T(8,128)(2,1)} %param.23) | copy-start | bytes 786436
  7.2 128.1 %all-gather.2.cloned.1.call-start = ((), (), s32[]{:S(2)}) async-start(), calls=%async_computation | async-start | bytes 2359296 | tf_op jit(solution)/shard_map/all_gather | solution.py:120
  10.5 16.8 %collective-permute-start = (bf16[1,64,128]{2,1,0:T(8,128)(2,1)S(1)}, bf16[1,64,128]{2,1,0:T(8,128)(2,1)S(1)}, u32[]{:S(2)}, u32[]{:S(2)}) collective-permute-start(bf16[1,64,128]{2,1,0:T(8,128)(2,1)S(1)} %convert_bitcast_fusion.3), channel_id=1, source_target_pairs={{0,8},{8,16},{16,24},{24,32},{32,40},{40,48},{48,56},{56,64},{64,7... | collective-permute-start | bytes 49160 | tf_op jit(solution)/shard_map/ppermute | solution.py:28
  12.4 16.2 %collective-permute-start.1 = (bf16[1,64,128]{2,1,0:T(8,128)(2,1)S(1)}, bf16[1,64,128]{2,1,0:T(8,128)(2,1)S(1)}, u32[]{:S(2)}, u32[]{:S(2)}) collective-permute-start(bf16[1,64,128]{2,1,0:T(8,128)(2,1)S(1)} %convert_bitcast_fusion.3), channel_id=1, source_target_pairs={{8,0},{16,8},{24,16},{32,24},{40,32},{48,40},{56,48},{64,56},{72,6... | collective-permute-start | bytes 49160 | tf_op jit(solution)/shard_map/ppermute | solution.py:29
  30.2 107.8 %copy-start.13 = (bf16[1024,128]{1,0:T(8,128)(2,1)}, bf16[1024,128]{1,0:T(8,128)(2,1)S(1)}, u32[]{:S(2)}) copy-start(bf16[1024,128]{1,0:T(8,128)(2,1)S(1)} %fusion.38) | copy-start | bytes 786436
  114.3 24.5 %copy-start.7 = (bf16[1,1024,128]{2,1,0:T(8,128)(2,1)S(1)}, bf16[1,1024,128]{2,1,0:T(8,128)(2,1)}, u32[]{:S(2)}) copy-start(bf16[1,1024,128]{2,1,0:T(8,128)(2,1)} %param.24) | copy-start | bytes 786436
  138.0 1.6 copy-start.10
  147.9 2.0 %copy-start.2 = (bf16[1,1024,128]{2,1,0:T(8,128)(2,1)S(1)}, bf16[1,1024,128]{2,1,0:T(8,128)(2,1)}, u32[]{:S(2)}) copy-start(bf16[1,1024,128]{2,1,0:T(8,128)(2,1)} %param.17) | copy-start | bytes 786436
  148.0 2.0 %copy-start.5 = (bf16[1,1024,1024]{2,1,0:T(8,128)(2,1)S(1)}, bf16[1,1024,1024]{2,1,0:T(8,128)(2,1)}, u32[]{:S(2)}) copy-start(bf16[1,1024,1024]{2,1,0:T(8,128)(2,1)} %all-gather.2.cloned.1.call-done) | copy-start | bytes 6291460
  148.0 2.0 %copy-start.8 = (bf16[1,1024,128]{2,1,0:T(8,128)(2,1)S(1)}, bf16[1,1024,128]{2,1,0:T(8,128)(2,1)}, u32[]{:S(2)}) copy-start(bf16[1,1024,128]{2,1,0:T(8,128)(2,1)} %param.19) | copy-start | bytes 786436
  148.0 2.0 %copy-start.9 = (bf16[1,1024,128]{2,1,0:T(8,128)(2,1)S(1)}, bf16[1,1024,128]{2,1,0:T(8,128)(2,1)}, u32[]{:S(2)}) copy-start(bf16[1,1024,128]{2,1,0:T(8,128)(2,1)} %param.18) | copy-start | bytes 786436
  151.8 18.1 %copy-start.6 = (bf16[1024,128]{1,0:T(8,128)(2,1)}, bf16[1024,128]{1,0:T(8,128)(2,1)S(1)}, u32[]{:S(2)}) copy-start(bf16[1024,128]{1,0:T(8,128)(2,1)S(1)} %get-tuple-element.25) | copy-start | bytes 786436
  152.1 15.7 %collective-permute-start.2 = (f32[1,64,128]{2,1,0:T(8,128)S(1)}, f32[1,64,128]{2,1,0:T(8,128)S(1)}, u32[]{:S(2)}, u32[]{:S(2)}) collective-permute-start(f32[1,64,128]{2,1,0:T(8,128)S(1)} %bitcast.158), channel_id=1, source_target_pairs={{0,8},{8,16},{16,24},{24,32},{32,40},{40,48},{48,56},{56,64},{64,7... | collective-permute-start | bytes 98312 | tf_op jit(solution)/shard_map/ppermute | solution.py:28
  154.1 13.9 %collective-permute-start.3 = (f32[1,64,128]{2,1,0:T(8,128)S(1)}, f32[1,64,128]{2,1,0:T(8,128)S(1)}, u32[]{:S(2)}, u32[]{:S(2)}) collective-permute-start(f32[1,64,128]{2,1,0:T(8,128)S(1)} %bitcast.159), channel_id=1, source_target_pairs={{8,0},{16,8},{24,16},{32,24},{40,32},{48,40},{56,48},{64,56},{72,6... | collective-permute-start | bytes 98312 | tf_op jit(solution)/shard_map/ppermute | solution.py:29
Sparse Core Ops, SparseCore 0:
  11.3 124.0 all-gather.1
where the time goes:
time: 178 us
  blocking collectives  77.9 us (44%)
  starting transfers between devices  31 us (17%)
  matrix products  23.6 us (13%)
  waiting for transfers between devices  23.3 us (13%)
  between operations  16.1 us (9%)
  other arithmetic  5.04 us (3%)
    psum x5, blocking collectives, over_axes(): value = lax.psum(value, axis)  77.9 us
    ppermute x2, starting transfers between devices, extended(): after = lax.ppermute(leading, axis, down)  27.1 us
    all_gather x1, waiting for transfers between devices, local_gradient(): gathered = lax.all_gather(tokens, TP, axis=1, tiled=True)  21.1 us
    dot_general x4, matrix products, place_rows(): lax.dot_general(matrix, values, (((0,), (0,)), ((), ())), precision=lax.P...  7.71 us
    dot_general x5, matrix products, contract(): lax.dot_general(left, right, (((left_dim,), (right_dim,)), ((), ())), pre...  7.34 us
    ppermute x2, starting transfers between devices, extended(): before = lax.ppermute(last, axis, up)  3.84 us
    dot_general x2, matrix products, head_grad(): jnp.dot(score_grad, key_head, preferred_element_type=jnp.float32)  3.83 us
  transfers between devices with their start and end apart: 5, of which 3 were waited for; matrix products, arithmetic and copies ran while one was open for 6% of the time, Pallas kernels for 0%

commit v1 on v0

--- a/solution.py
+++ b/solution.py
@@ -117,7 +117,9 @@
     model_width = weights_new.shape[0]
     query_weight = (weights_new * model_width ** (-0.5)).astype(jnp.bfloat16)
     joined = jnp.concatenate([query_weight, key_weight, value_weight], axis=1)
-    gathered = lax.all_gather(tokens, TP, axis=1, tiled=True)
+    gathered = jnp.concatenate(
+        lax.all_to_all(jnp.stack([tokens] * lax.axis_size(TP)), TP, 0, 0), axis=1
+    )
     projected = jnp.dot(gathered[0], joined, preferred_element_type=jnp.float32).astype(
         jnp.bfloat16
     )[None][0]

time: 178 us -> 223 us (1.25)
  the two profiles are of different devices: /device:TPU:8 before, /device:TPU:487 now
where the time goes in v1:
time: 223 us
  blocking collectives  77.9 us (35%)
  waiting for transfers between devices  72.3 us (32%)
  starting transfers between devices  42.3 us (19%)
  matrix products  20 us (9%)
  other arithmetic  4.42 us (2%)
  local copies, waits for them, and re-layouts  3.45 us (2%)
  between operations  2.69 us (1%)
    psum x5, blocking collectives, over_axes(): value = lax.psum(value, axis)  77.9 us
    ppermute x2, waiting for transfers between devices, extended(): after = lax.ppermute(leading, axis, down)  50.1 us
    ppermute x2, starting transfers between devices, extended(): before = lax.ppermute(last, axis, up)  24.4 us
    ppermute x2, waiting for transfers between devices, extended(): before = lax.ppermute(last, axis, up)  22.2 us
    all_to_all x1, starting transfers between devices, local_gradient(): lax.all_to_all(jnp.stack([tokens] * lax.axis_size(TP)), TP, 0, 0)  14.1 us
    dot_general x5, matrix products, contract(): lax.dot_general(left, right, (((left_dim,), (right_dim,)), ((), ())), pre...  7.36 us
    dot_general x4, matrix products, place_rows(): lax.dot_general(matrix, values, (((0,), (0,)), ((), ())), precision=lax.P...  5.72 us
  transfers between devices with their start and end apart: 5, of which 3 were waited for; matrix products, arithmetic and copies ran while one was open for 3% of the time, Pallas kernels for 0%

profile of v1, /device:TPU:487, one launch (start us, length us, event | category | flops | bytes accessed | tf_op | source)
XLA Modules:
  0.0 223.0 jit_solution(3579628218295752636)
XLA Ops:
  0.6 0.0 copy-start
  0.6 0.0 copy-start.3
  0.7 0.0 copy-start.4
  0.7 2.7 %stack.2 = bf16[8,1,128,1024]{3,2,1,0:T(8,128)(2,1)} broadcast(bf16[128,1024]{1,0:T(8,128)(2,1)} %bitcast.152), dimensions={2,3} | broadcast | bytes 2359296 | tf_op jit(solution)/shard_map/stack | solution.py:121
  3.3 14.1 %all-to-all-start = ((bf16[8,1,128,1024]{3,2,1,0:T(8,128)(2,1)}), bf16[8,1,128,1024]{3,2,1,0:T(8,128)(2,1)S(1)}, u32[]{:S(2)}, u32[]{:S(2)}) async-start(bf16[8,1,128,1024]{3,2,1,0:T(8,128)(2,1)} %stack.2), calls=%async_computation | async-start | bytes 4194304 | tf_op jit(solution)/shard_map/all_to_all | solution.py:121
  17.4 0.7 constant_dynamic-slice_fusion.1
  18.1 0.0 copy-done
  18.2 0.5 fusion.50
  18.7 7.5 %collective-permute-start = (bf16[1,64,128]{2,1,0:T(8,128)(2,1)S(1)}, bf16[1,64,128]{2,1,0:T(8,128)(2,1)S(1)}, u32[]{:S(2)}, u32[]{:S(2)}) collective-permute-start(bf16[1,64,128]{2,1,0:T(8,128)(2,1)S(1)} %convert_bitcast_fusion.3), channel_id=1, source_target_pairs={{0,8},{8,16},{16,24},{24,32},{32,40},{40,48},{48,56},{56,64},{64,7... | collective-permute-start | bytes 49160 | tf_op jit(solution)/shard_map/ppermute | solution.py:28
  26.2 1.9 collective-permute-start.1
  28.2 0.1 pad_add_fusion
  28.2 22.2 %collective-permute-done = bf16[1,64,128]{2,1,0:T(8,128)(2,1)S(1)} collective-permute-done((bf16[1,64,128]{2,1,0:T(8,128)(2,1)S(1)}, bf16[1,64,128]{2,1,0:T(8,128)(2,1)S(1)}, u32[]{:S(2)}, u32[]{:S(2)}) %collective-permute-start) | collective-permute-done | bytes 16416 | tf_op jit(solution)/shard_map/ppermute | solution.py:28
  50.5 39.4 %collective-permute-done.1 = bf16[1,64,128]{2,1,0:T(8,128)(2,1)S(1)} collective-permute-done((bf16[1,64,128]{2,1,0:T(8,128)(2,1)S(1)}, bf16[1,64,128]{2,1,0:T(8,128)(2,1)S(1)}, u32[]{:S(2)}, u32[]{:S(2)}) %collective-permute-start.1) | collective-permute-done | bytes 16416 | tf_op jit(solution)/shard_map/ppermute | solution.py:29
  89.9 0.6 fusion.26
  90.5 0.0 copy-start.10
  90.5 2.0 multiply_reduce_fusion
  92.5 0.0 copy-done.10
  92.5 6.7 %psum.35 = f32[]{:T(128)} all-reduce(f32[]{:T(128)} %get-tuple-element.27), channel_id=1, replica_groups=mesh['blk_0'=4,'blk_1'=8,'blk_2'=2,'tp_0'=2,'tp_1'=4] {'blk_0'}, use_global_device_ids=true, to_apply=%region_7.8 | all-reduce | flops 1 | bytes 8 | tf_op jit(solution)/shard_map/psum | solution.py:17
  99.1 34.6 %psum.36 = f32[]{:T(128)} all-reduce(f32[]{:T(128)} %psum.35), channel_id=1, replica_groups=mesh['blk_0'=4,'blk_1'=8,'blk_2'=2,'tp_0'=2,'tp_1'=4] {'blk_1'}, use_global_device_ids=true, to_apply=%region_8.9 | all-reduce | flops 1 | bytes 8 | tf_op jit(solution)/shard_map/psum | solution.py:17
  133.7 0.9 fusion.54
  134.6 14.8 %psum.37 = f32[]{:T(128)} all-reduce(f32[]{:T(128)} %psum.36), channel_id=1, replica_groups=mesh['blk_0'=4,'blk_1'=8,'blk_2'=2,'tp_0'=2,'tp_1'=4] {'blk_2'}, use_global_device_ids=true, to_apply=%region_9.10 | all-reduce | flops 1 | bytes 8 | tf_op jit(solution)/shard_map/psum | solution.py:17
  149.4 0.9 multiply_convert_fusion
  150.3 13.1 %psum.38 = f32[]{:T(128)} all-reduce(f32[]{:T(128)} %psum.37), channel_id=1, replica_groups=mesh['blk_0'=4,'blk_1'=8,'blk_2'=2,'tp_0'=2,'tp_1'=4] {'tp_0'}, use_global_device_ids=true, to_apply=%region_10.11 | all-reduce | flops 1 | bytes 8 | tf_op jit(solution)/shard_map/psum | solution.py:17
  163.4 0.1 pad_add_fusion.1
  163.5 8.7 %psum.39 = f32[]{:T(128)} all-reduce(f32[]{:T(128)} %psum.38), channel_id=1, replica_groups=mesh['blk_0'=4,'blk_1'=8,'blk_2'=2,'tp_0'=2,'tp_1'=4] {'tp_1'}, use_global_device_ids=true, to_apply=%region_11.12 | all-reduce | flops 1 | bytes 8 | tf_op jit(solution)/shard_map/psum | solution.py:17
  172.9 0.0 all-to-all-done
  172.9 0.0 copy-start.6
  172.9 2.2 fusion.22
  175.1 0.0 copy-start.9
  175.1 0.8 fusion.72
  175.9 0.8 fusion.63
  176.7 0.0 copy-done.9
  176.7 1.3 fusion.12
  177.9 2.4 %fusion.9 = (f32[1024]{0:T(1024)S(1)}, f32[1024]{0:T(1024)S(1)}) fusion(f32[1024,1024]{0,1:T(8,128)S(1)} %get-tuple-element.23, f32[1024]{0:T(1024)S(1)} %get-tuple-element.12, s32[1024]{0:T(1024)S(1)} %bitcast.159, f32[1024]{0:T(1024)S(1)} %get-tuple-element.13, f32[1024,1024]{0,1:T(8,128)S(1)} %fusion.72), kind=kLoop, calls=%fused_computation.17 | loop fusion | flops 9435136 | bytes 8409088 | tf_op jit(solution)/shard_map/reduce_sum | solution.py:88
  180.4 2.8 %fusion.4 = (f32[1024]{0:T(1024)S(1)}, f32[1024]{0:T(1024)S(1)}, f32[1024,1024]{1,0:T(8,128)S(1)}) fusion(f32[1024]{0:T(1024)S(1)} %get-tuple-element.10, f32[1024]{0:T(1024)S(1)} %get-tuple-element.12, f32[1024,1024]{0,1:T(8,128)S(1)} %get-tuple-element.23, s32[1024]{0:T(1024)S(1)} %bitcast.160, f32[1024,1024]{1,0:T(8,128)S(1)} %fusion.63, ...), kind=kOutput, calls=%fused_computation.10 | convolution fusion | flops 147847168 | bytes 17203200 | tf_op jit(solution)/shard_map/dot_general | solution.py:35
  183.1 1.9 fusion.29
  185.1 0.0 copy-start.2
  185.1 0.0 copy-start.7
  185.1 0.0 copy-start.8
  185.1 1.9 fusion.32
  187.1 1.8 fusion.57
  188.9 0.4 fusion.59
  189.3 16.8 %collective-permute-start.2 = (f32[1,64,128]{2,1,0:T(8,128)S(1)}, f32[1,64,128]{2,1,0:T(8,128)S(1)}, u32[]{:S(2)}, u32[]{:S(2)}) collective-permute-start(f32[1,64,128]{2,1,0:T(8,128)S(1)} %bitcast.149), channel_id=1, source_target_pairs={{0,8},{8,16},{16,24},{24,32},{32,40},{40,48},{48,56},{56,64},{64,7... | collective-permute-start | bytes 98312 | tf_op jit(solution)/shard_map/ppermute | solution.py:28
  206.1 1.9 collective-permute-start.3
  208.1 1.4 fusion.36
  209.4 0.0 collective-permute-done.2
  209.5 10.6 %collective-permute-done.3 = f32[1,64,128]{2,1,0:T(8,128)S(1)} collective-permute-done((f32[1,64,128]{2,1,0:T(8,128)S(1)}, f32[1,64,128]{2,1,0:T(8,128)S(1)}, u32[]{:S(2)}, u32[]{:S(2)}) %collective-permute-start.3) | collective-permute-done | bytes 32800 | tf_op jit(solution)/shard_map/ppermute | solution.py:29
  220.1 1.8 fusion.37
  (15 shorter events, 0.1 us)
Async XLA Ops:
  0.6 17.5 %copy-start = (f32[1,1024,128]{2,1,0:T(8,128)S(1)}, f32[1,1024,128]{2,1,0:T(8,128)}, u32[]{:S(2)}) copy-start(f32[1,1024,128]{2,1,0:T(8,128)} %param.13) | copy-start | bytes 1572868
  0.6 17.5 %copy-start.3 = (bf16[1,1024,128]{2,1,0:T(8,128)(2,1)S(1)}, bf16[1,1024,128]{2,1,0:T(8,128)(2,1)}, u32[]{:S(2)}) copy-start(bf16[1,1024,128]{2,1,0:T(8,128)(2,1)} %param.14) | copy-start | bytes 786436
  0.7 17.5 %copy-start.4 = (bf16[1,1024,128]{2,1,0:T(8,128)(2,1)S(1)}, bf16[1,1024,128]{2,1,0:T(8,128)(2,1)}, u32[]{:S(2)}) copy-start(bf16[1,1024,128]{2,1,0:T(8,128)(2,1)} %param.15) | copy-start | bytes 786436
  0.7 17.5 %copy-start.1 = (bf16[1,1024,128]{2,1,0:T(8,128)(2,1)S(1)}, bf16[1,1024,128]{2,1,0:T(8,128)(2,1)}, u32[]{:S(2)}) copy-start(bf16[1,1024,128]{2,1,0:T(8,128)(2,1)} %param.16) | copy-start | bytes 786436
  3.3 169.5 %all-to-all-start = ((bf16[8,1,128,1024]{3,2,1,0:T(8,128)(2,1)}), bf16[8,1,128,1024]{3,2,1,0:T(8,128)(2,1)S(1)}, u32[]{:S(2)}, u32[]{:S(2)}) async-start(bf16[8,1,128,1024]{3,2,1,0:T(8,128)(2,1)} %stack.2), calls=%async_computation | async-start | bytes 4194304 | tf_op jit(solution)/shard_map/all_to_all | solution.py:121
  18.7 31.8 %collective-permute-start = (bf16[1,64,128]{2,1,0:T(8,128)(2,1)S(1)}, bf16[1,64,128]{2,1,0:T(8,128)(2,1)S(1)}, u32[]{:S(2)}, u32[]{:S(2)}) collective-permute-start(bf16[1,64,128]{2,1,0:T(8,128)(2,1)S(1)} %convert_bitcast_fusion.3), channel_id=1, source_target_pairs={{0,8},{8,16},{16,24},{24,32},{32,40},{40,48},{48,56},{56,64},{64,7... | collective-permute-start | bytes 49160 | tf_op jit(solution)/shard_map/ppermute | solution.py:28
  26.2 63.7 %collective-permute-start.1 = (bf16[1,64,128]{2,1,0:T(8,128)(2,1)S(1)}, bf16[1,64,128]{2,1,0:T(8,128)(2,1)S(1)}, u32[]{:S(2)}, u32[]{:S(2)}) collective-permute-start(bf16[1,64,128]{2,1,0:T(8,128)(2,1)S(1)} %convert_bitcast_fusion.3), channel_id=1, source_target_pairs={{8,0},{16,8},{24,16},{32,24},{40,32},{48,40},{56,48},{64,56},{72,6... | collective-permute-start | bytes 49160 | tf_op jit(solution)/shard_map/ppermute | solution.py:29
  90.5 2.0 copy-start.10
  172.9 3.0 %copy-start.6 = (bf16[1,1024,128]{2,1,0:T(8,128)(2,1)S(1)}, bf16[1,1024,128]{2,1,0:T(8,128)(2,1)}, u32[]{:S(2)}) copy-start(bf16[1,1024,128]{2,1,0:T(8,128)(2,1)} %param.24) | copy-start | bytes 786436
  175.1 1.6 copy-start.9
  185.1 2.0 copy-start.2
  185.1 2.0 copy-start.7
  185.1 2.0 copy-start.8
  188.9 33.0 %copy-start.5 = (bf16[1024,128]{1,0:T(8,128)(2,1)}, bf16[1024,128]{1,0:T(8,128)(2,1)S(1)}, u32[]{:S(2)}) copy-start(bf16[1024,128]{1,0:T(8,128)(2,1)S(1)} %get-tuple-element.25) | copy-start | bytes 786436
  189.3 20.2 %collective-permute-start.2 = (f32[1,64,128]{2,1,0:T(8,128)S(1)}, f32[1,64,128]{2,1,0:T(8,128)S(1)}, u32[]{:S(2)}, u32[]{:S(2)}) collective-permute-start(f32[1,64,128]{2,1,0:T(8,128)S(1)} %bitcast.149), channel_id=1, source_target_pairs={{0,8},{8,16},{16,24},{24,32},{32,40},{40,48},{48,56},{56,64},{64,7... | collective-permute-start | bytes 98312 | tf_op jit(solution)/shard_map/ppermute | solution.py:28
  206.1 13.9 %collective-permute-start.3 = (f32[1,64,128]{2,1,0:T(8,128)S(1)}, f32[1,64,128]{2,1,0:T(8,128)S(1)}, u32[]{:S(2)}, u32[]{:S(2)}) collective-permute-start(f32[1,64,128]{2,1,0:T(8,128)S(1)} %bitcast.150), channel_id=1, source_target_pairs={{8,0},{16,8},{24,16},{32,24},{40,32},{48,40},{56,48},{64,56},{72,6... | collective-permute-start | bytes 98312 | tf_op jit(solution)/shard_map/ppermute | solution.py:29
